TPU v7x, 32 devices: a whole 2x2x4 slice. The times are simulated.
32 devices in a mesh: fsdp: 4 (over y, x), dp: 8 (over z, core).
Axes of the slice: x: 2, y: 2, z: 4, core: 2. Of those that a mesh axis runs over, the one named last changes fastest.
Arguments:
- tokens: bfloat16 [16384, 960], P(('fsdp', 'dp')), may hold values from -6 to 6
- span_table: int32 [8, 8], P('dp'), may hold values from 0 to 7, as said below
- w_query: bfloat16 [960, 960], P('fsdp'), may hold values from -0.1875 to 0.1875
- w_key: bfloat16 [960, 320], P('fsdp'), may hold values from -0.1875 to 0.1875
- w_value: bfloat16 [960, 320], P('fsdp'), may hold values from -0.1875 to 0.1875
- w_out: bfloat16 [960, 960], P('fsdp'), may hold values from -3.5 to 3.5
- w_gate: bfloat16 [960, 2560], P('fsdp'), may hold values from -0.1875 to 0.1875
- w_up: bfloat16 [960, 2560], P('fsdp'), may hold values from -0.1875 to 0.1875
- w_down: bfloat16 [2560, 960], P('fsdp'), may hold values from -0.125 to 0.125
- gain_attn: bfloat16 [960], P('fsdp'), may hold values from 0.099609375 to 1.8984375
- gain_ffn: bfloat16 [960], P('fsdp'), may hold values from 0.099609375 to 1.8984375
- cotangent: bfloat16 [16384, 960], P(('fsdp', 'dp')), may hold values from -6 to 6
Outputs:
- output: bfloat16 [16384, 960], P(('fsdp', 'dp'))
- grad_tokens: float32 [16384, 960], P(('fsdp', 'dp'))
- grad_w_query: float32 [960, 960], P('fsdp')
- grad_w_key: float32 [960, 320], P('fsdp')
- grad_w_value: float32 [960, 320], P('fsdp')
- grad_w_out: float32 [960, 960], P('fsdp')
- grad_w_gate: float32 [960, 2560], P('fsdp')
- grad_w_up: float32 [960, 2560], P('fsdp')
- grad_w_down: float32 [2560, 960], P('fsdp')
- grad_gain_attn: float32 [960], P('fsdp')
- grad_gain_ffn: float32 [960], P('fsdp')
Inputs may be any that keep to these rules, and one draw needn't show every extreme that they name: `span_table`: each row is a permutation of the 8 blocks of a sequence over the slots.
All inputs are finite; a program needn't handle non-finite values.
Results may differ from a plain program's by a relative error of at most 0.022.
Values may be sent and summed in bfloat16 or wider, within the bound.
A program may use at most 192 MiB of HBM per device.

v0:
```python
import jax
import jax.numpy as jnp
from jax import lax
from jax.sharding import PartitionSpec as P

HEADS = 15
KV_HEADS = 5
HEAD_DIM = 64


epsilon = 1e-05
rope_base = 100000.0


def rope_tables(places, head_dim):
    half_dim = head_dim // 2
    rates = rope_base ** (-2.0 * jnp.arange(half_dim, dtype=jnp.float32) / head_dim)
    angles = places.astype(jnp.float32)[:, None] * rates[None, :]
    return (jnp.cos(angles)[:, None, :], jnp.sin(angles)[:, None, :])


def rotate(field, cosine, sine_part):
    half_dim = field.shape[-1] // 2
    first = field[..., :half_dim]
    second = field[..., half_dim:]
    return jnp.concatenate(
        [first * cosine - second * sine_part, second * cosine + first * sine_part], axis=-1
    )


def rms_scale(values):
    return lax.rsqrt(jnp.mean(values * values, axis=-1, keepdims=True) + epsilon)


def norm_back(grad_normed, values, scale_rows, gain):
    scaled = values * scale_rows
    weighted = grad_normed * gain
    grad_values = scale_rows * (
        weighted - scaled * jnp.mean(weighted * scaled, axis=-1, keepdims=True)
    )
    return (grad_values, jnp.sum(grad_normed * scaled, axis=0))


def matmul(left, right):
    return jnp.dot(left, right, preferred_element_type=jnp.float32)


def outer(left, right):
    return jnp.einsum("rd,re->de", left, right, preferred_element_type=jnp.float32)


def inner_back(grad_rows, weight):
    return jnp.einsum("re,de->rd", grad_rows, weight, preferred_element_type=jnp.float32)


def keys_by_head(gathered, groups, seqs):
    spread = gathered.reshape(groups, seqs, -1, KV_HEADS, HEAD_DIM)
    return spread.transpose(3, 1, 0, 2, 4).reshape(KV_HEADS, seqs, -1, HEAD_DIM)


def on_device(
    tokens,
    span_table,
    w_query,
    w_key,
    w_value,
    w_out,
    w_gate,
    w_up,
    w_down,
    gain_attn,
    gain_ffn,
    cotangent,
):
    groups = lax.axis_size("fsdp")
    index = lax.axis_index("fsdp")
    rows = tokens.shape[0]
    seqs = span_table.shape[0]
    span = rows // (2 * seqs)
    per_kv = HEADS // KV_HEADS
    scale = HEAD_DIM ** (-0.5)
    full = (
        lax.all_gather(w_query, "fsdp", axis=0, tiled=True),
        lax.all_gather(w_key, "fsdp", axis=0, tiled=True),
        lax.all_gather(w_value, "fsdp", axis=0, tiled=True),
        lax.all_gather(w_out, "fsdp", axis=0, tiled=True),
        lax.all_gather(w_gate, "fsdp", axis=0, tiled=True),
        lax.all_gather(w_up, "fsdp", axis=0, tiled=True),
        lax.all_gather(w_down, "fsdp", axis=0, tiled=True),
        lax.all_gather(gain_attn, "fsdp", axis=0, tiled=True),
        lax.all_gather(gain_ffn, "fsdp", axis=0, tiled=True),
    )
    (
        query_full,
        key_full,
        value_full,
        out_full,
        gate_full,
        up_full,
        down_full,
        attn_gain,
        ffn_gain,
    ) = full
    attn_gain = attn_gain.astype(jnp.float32)
    ffn_gain = ffn_gain.astype(jnp.float32)
    offsets = jnp.arange(span, dtype=jnp.int32)
    mine = lax.dynamic_slice_in_dim(span_table, 2 * index, 2, 1)
    query_place = (mine[:, :, None] * span + offsets).reshape(seqs, 2 * span)
    key_place = (span_table.reshape(seqs, groups, 2)[:, :, :, None] * span + offsets).reshape(
        seqs, -1
    )
    allowed = query_place[:, None, :, None] >= key_place[:, None, None, :]
    cosine, sine_part = rope_tables(query_place.reshape(-1), HEAD_DIM)
    inputs = tokens.astype(jnp.float32)
    scale_one = rms_scale(inputs)
    normed_one = (inputs * scale_one * attn_gain).astype(jnp.bfloat16)
    query_rows = rotate(
        matmul(normed_one, query_full).reshape(rows, HEADS, HEAD_DIM), cosine, sine_part
    ).astype(jnp.bfloat16)
    key_rows = (
        rotate(matmul(normed_one, key_full).reshape(rows, KV_HEADS, HEAD_DIM), cosine, sine_part)
        .astype(jnp.bfloat16)
        .reshape(rows, -1)
    )
    value_rows = matmul(normed_one, value_full).astype(jnp.bfloat16)
    key_all, value_all = (
        lax.all_gather(key_rows, "fsdp", axis=0, tiled=True),
        lax.all_gather(value_rows, "fsdp", axis=0, tiled=True),
    )
    key_heads = keys_by_head(key_all, groups, seqs)
    value_heads = keys_by_head(value_all, groups, seqs)
    query_heads = query_rows.reshape(seqs, 2 * span, KV_HEADS, per_kv, HEAD_DIM).transpose(
        2, 0, 3, 1, 4
    )

    def forward_head(operands):
        query, keys, values = operands
        raw_scores = (
            jnp.einsum("sgqd,skd->sgqk", query, keys, preferred_element_type=jnp.float32) * scale
        )
        scores = jnp.where(allowed, raw_scores, -1e30)
        row_max = jnp.max(scores, axis=-1, keepdims=True)
        powers = jnp.exp(scores - row_max)
        totals = jnp.sum(powers, axis=-1, keepdims=True)
        weights = (powers / totals).astype(jnp.bfloat16)
        mixed = jnp.einsum("sgqk,skd->sgqd", weights, values, preferred_element_type=jnp.float32)
        return (mixed, row_max + jnp.log(totals))

    mixed_heads, log_sums = lax.map(forward_head, (query_heads, key_heads, value_heads))
    attended = (
        mixed_heads.transpose(1, 3, 0, 2, 4).reshape(rows, HEADS * HEAD_DIM).astype(jnp.bfloat16)
    )
    hidden = inputs + matmul(attended, out_full)
    scale_two = rms_scale(hidden)
    normed_two = (hidden * scale_two * ffn_gain).astype(jnp.bfloat16)
    gate = matmul(normed_two, gate_full)
    upward = matmul(normed_two, up_full)
    sigma = jax.nn.sigmoid(gate)
    activated = gate * sigma
    inner = (activated * upward).astype(jnp.bfloat16)
    output = (hidden + matmul(inner, down_full)).astype(jnp.bfloat16)
    back = (
        lax.all_gather(w_query, "fsdp", axis=0, tiled=True),
        lax.all_gather(w_key, "fsdp", axis=0, tiled=True),
        lax.all_gather(w_value, "fsdp", axis=0, tiled=True),
        lax.all_gather(w_out, "fsdp", axis=0, tiled=True),
        lax.all_gather(w_gate, "fsdp", axis=0, tiled=True),
        lax.all_gather(w_up, "fsdp", axis=0, tiled=True),
        lax.all_gather(w_down, "fsdp", axis=0, tiled=True),
        lax.all_gather(gain_attn, "fsdp", axis=0, tiled=True),
        lax.all_gather(gain_ffn, "fsdp", axis=0, tiled=True),
    )
    query_back, key_back, value_back, out_back, gate_back, up_back, down_back = back[:7]
    grad_out = cotangent.astype(jnp.float32)
    grad_w_down = outer(inner, cotangent)
    grad_inner = inner_back(cotangent, down_back)
    grad_gate = (grad_inner * upward * sigma * (1.0 + gate * (1.0 - sigma))).astype(jnp.bfloat16)
    grad_up = (grad_inner * activated).astype(jnp.bfloat16)
    grad_w_gate = outer(normed_two, grad_gate)
    grad_w_up = outer(normed_two, grad_up)
    grad_normed_two = inner_back(grad_gate, gate_back) + inner_back(grad_up, up_back)
    grad_hidden_norm, grad_gain_ffn = norm_back(grad_normed_two, hidden, scale_two, ffn_gain)
    grad_hidden = grad_out + grad_hidden_norm
    grad_branch = grad_hidden.astype(jnp.bfloat16)
    grad_w_out = outer(attended, grad_branch)
    grad_attended = inner_back(grad_branch, out_back).astype(jnp.bfloat16)
    grad_heads = grad_attended.reshape(seqs, 2 * span, KV_HEADS, per_kv, HEAD_DIM).transpose(
        2, 0, 3, 1, 4
    )

    def backward_head(operands):
        query, keys, values, grad_mixed, log_sum = operands
        raw_scores = (
            jnp.einsum("sgqd,skd->sgqk", query, keys, preferred_element_type=jnp.float32) * scale
        )
        scores = jnp.where(allowed, raw_scores, -1e30)
        probs = jnp.exp(scores - log_sum)
        weights = probs.astype(jnp.bfloat16)
        grad_values = jnp.einsum(
            "sgqk,sgqd->skd", weights, grad_mixed, preferred_element_type=jnp.float32
        )
        grad_probs = jnp.einsum(
            "sgqd,skd->sgqk", grad_mixed, values, preferred_element_type=jnp.float32
        )
        centred = jnp.sum(probs * grad_probs, axis=-1, keepdims=True)
        grad_scores = (probs * (grad_probs - centred) * scale).astype(jnp.bfloat16)
        grad_query = jnp.einsum(
            "sgqk,skd->sgqd", grad_scores, keys, preferred_element_type=jnp.float32
        )
        grad_keys = jnp.einsum(
            "sgqk,sgqd->skd", grad_scores, query, preferred_element_type=jnp.float32
        )
        return (grad_query, grad_keys, grad_values)

    grad_query_heads, grad_key_heads, grad_value_heads = lax.map(
        backward_head, (query_heads, key_heads, value_heads, grad_heads, log_sums)
    )

    def to_gathered(field):
        spread = field.reshape(KV_HEADS, seqs, groups, 2 * span, HEAD_DIM)
        return spread.transpose(2, 1, 3, 0, 4).reshape(groups * rows, KV_HEADS * HEAD_DIM)

    grad_key_turned, grad_value_sum = (
        lax.psum_scatter(
            to_gathered(grad_key_heads).astype(jnp.bfloat16),
            "fsdp",
            scatter_dimension=0,
            tiled=True,
        ).astype(jnp.float32),
        lax.psum_scatter(
            to_gathered(grad_value_heads).astype(jnp.bfloat16),
            "fsdp",
            scatter_dimension=0,
            tiled=True,
        ).astype(jnp.float32),
    )
    grad_key_rows = (
        rotate(grad_key_turned.reshape(rows, KV_HEADS, HEAD_DIM), cosine, -sine_part)
        .reshape(rows, -1)
        .astype(jnp.bfloat16)
    )
    grad_query_turned = grad_query_heads.transpose(1, 3, 0, 2, 4).reshape(rows, HEADS, HEAD_DIM)
    grad_query_rows = (
        rotate(grad_query_turned, cosine, -sine_part).reshape(rows, -1).astype(jnp.bfloat16)
    )
    grad_value_rows = grad_value_sum.astype(jnp.bfloat16)
    grad_w_query = outer(normed_one, grad_query_rows)
    grad_w_key = outer(normed_one, grad_key_rows)
    grad_w_value = outer(normed_one, grad_value_rows)
    grad_normed_one = (
        inner_back(grad_query_rows, query_back)
        + inner_back(grad_key_rows, key_back)
        + inner_back(grad_value_rows, value_back)
    )
    grad_input_norm, grad_gain_attn = norm_back(grad_normed_one, inputs, scale_one, attn_gain)
    grad_tokens = grad_hidden + grad_input_norm
    owned = (
        lax.psum_scatter(
            grad_w_query.astype(jnp.bfloat16), "fsdp", scatter_dimension=0, tiled=True
        ).astype(jnp.float32),
        lax.psum_scatter(
            grad_w_key.astype(jnp.bfloat16), "fsdp", scatter_dimension=0, tiled=True
        ).astype(jnp.float32),
        lax.psum_scatter(
            grad_w_value.astype(jnp.bfloat16), "fsdp", scatter_dimension=0, tiled=True
        ).astype(jnp.float32),
        lax.psum_scatter(
            grad_w_out.astype(jnp.bfloat16), "fsdp", scatter_dimension=0, tiled=True
        ).astype(jnp.float32),
        lax.psum_scatter(
            grad_w_gate.astype(jnp.bfloat16), "fsdp", scatter_dimension=0, tiled=True
        ).astype(jnp.float32),
        lax.psum_scatter(
            grad_w_up.astype(jnp.bfloat16), "fsdp", scatter_dimension=0, tiled=True
        ).astype(jnp.float32),
        lax.psum_scatter(
            grad_w_down.astype(jnp.bfloat16), "fsdp", scatter_dimension=0, tiled=True
        ).astype(jnp.float32),
        lax.psum_scatter(
            grad_gain_attn.astype(jnp.bfloat16), "fsdp", scatter_dimension=0, tiled=True
        ).astype(jnp.float32),
        lax.psum_scatter(
            grad_gain_ffn.astype(jnp.bfloat16), "fsdp", scatter_dimension=0, tiled=True
        ).astype(jnp.float32),
    )
    summed = (
        lax.psum(owned[0].astype(jnp.bfloat16), "dp").astype(jnp.float32),
        lax.psum(owned[1].astype(jnp.bfloat16), "dp").astype(jnp.float32),
        lax.psum(owned[2].astype(jnp.bfloat16), "dp").astype(jnp.float32),
        lax.psum(owned[3].astype(jnp.bfloat16), "dp").astype(jnp.float32),
        lax.psum(owned[4].astype(jnp.bfloat16), "dp").astype(jnp.float32),
        lax.psum(owned[5].astype(jnp.bfloat16), "dp").astype(jnp.float32),
        lax.psum(owned[6].astype(jnp.bfloat16), "dp").astype(jnp.float32),
        lax.psum(owned[7].astype(jnp.bfloat16), "dp").astype(jnp.float32),
        lax.psum(owned[8].astype(jnp.bfloat16), "dp").astype(jnp.float32),
    )
    return (
        output,
        grad_tokens,
        summed[0],
        summed[1],
        summed[2],
        summed[3],
        summed[4],
        summed[5],
        summed[6],
        summed[7],
        summed[8],
    )


def solution(mesh):
    return jax.shard_map(
        on_device,
        mesh=mesh,
        in_specs=(
            P(("fsdp", "dp"), None),
            P("dp", None),
            P("fsdp", None),
            P("fsdp", None),
            P("fsdp", None),
            P("fsdp", None),
            P("fsdp", None),
            P("fsdp", None),
            P("fsdp", None),
            P("fsdp"),
            P("fsdp"),
            P(("fsdp", "dp"), None),
        ),
        out_specs=(
            P(("fsdp", "dp"), None),
            P(("fsdp", "dp"), None),
            P("fsdp", None),
            P("fsdp", None),
            P("fsdp", None),
            P("fsdp", None),
            P("fsdp", None),
            P("fsdp", None),
            P("fsdp", None),
            P("fsdp"),
            P("fsdp"),
        ),
        check_vma=False,
    )
```

profile of v0, /device:TPU:0, one launch (start us, length us, event | category | flops | bytes accessed | tf_op | source)
XLA Modules:
  0.0 1192.5 jit_solution(17150730521787951973)
XLA Ops:
  12.5 11.3 all-reduce.9
  23.9 10.8 all-gather
  38.3 10.2 all-gather.1
  55.7 11.7 all-gather.12.cloned.1.call-done
  74.5 23.9 %all-gather.14.cloned.1.call-done = bf16[2048,320]{0,1:T(8,128)(2,1)} async-done(((bf16[512,320]{0,1:T(8,128)(2,1)}), bf16[2048,320]{0,1:T(8,128)(2,1)}) %all-gather.14.cloned.1.call-update) | async-done | bytes 1310736 | tf_op jit(solution)/shard_map/all_gather | solution.py:128
  106.5 28.1 %all-gather.10.cloned.1.call-done = bf16[960,960]{1,0:T(8,128)(2,1)} async-done(((bf16[240,960]{1,0:T(8,128)(2,1)}), bf16[960,960]{1,0:T(8,128)(2,1)}) %all-gather.10.cloned.1.call-update) | async-done | bytes 1843216 | tf_op jit(solution)/shard_map/all_gather | solution.py:83
  137.9 104.2 %while.30 = (s32[]{:T(128)}, bf16[5,1,3,512,64]{3,4,2,1,0:T(8,128)(2,1)}, f32[5,1,3,512,1]{3,2,4,1,0:T(4,128)S(1)}, bf16[5,1,3,512,64]{3,4,2,1,0:T(8,128)(2,1)S(...) while((s32[]{:T(128)}, ...), condition=%wide.region_4.5_spmd.clone.clone, body=%wide.region_1.4_spmd.clone.sunk.clone | while | flops 844102144 | bytes 43124832 | solution.py:149
  138.6 6.1 fusion.204
  144.7 6.8 fusion.205
  151.4 7.4 fusion.206
  159.5 5.9 fusion.204
  165.4 6.8 fusion.205
  172.2 7.4 fusion.206
  180.2 5.9 fusion.204
  186.1 6.8 fusion.205
  192.9 7.4 fusion.206
  200.9 5.9 fusion.204
  206.8 6.8 fusion.205
  213.6 7.4 fusion.206
  221.6 5.9 fusion.204
  227.5 6.8 fusion.205
  234.3 7.4 fusion.206
  246.9 7.8 fusion.127
  254.7 36.7 %all-gather.18.cloned.1.call-done = bf16[960,2560]{1,0:T(8,128)(2,1)} async-done(((bf16[240,2560]{1,0:T(8,128)(2,1)}), bf16[960,2560]{1,0:T(8,128)(2,1)}) %all-gather.18.cloned.1.call-update) | async-done | bytes 4915216 | tf_op jit(solution)/shard_map/all_gather | solution.py:87
  291.4 7.0 fusion.126
  298.5 53.5 %all-gather.22.cloned.1.call-done = bf16[2560,960]{0,1:T(8,128)(2,1)} async-done(((bf16[640,960]{0,1:T(8,128)(2,1)}), bf16[2560,960]{0,1:T(8,128)(2,1)}) %all-gather.22.cloned.1.call-update) | async-done | bytes 4915216 | tf_op jit(solution)/shard_map/all_gather | solution.py:89
  352.0 10.4 multiply_convert_fusion.1
  365.2 6.1 multiply_reduce_fusion.1
  375.3 290.0 %while.31 = (s32[]{:T(128)}, f32[5,1,3,512,64]{3,4,2,1,0:T(8,128)S(1)}, bf16[5,1,2048,64]{2,3,1,0:T(8,128)(2,1)}, bf16[5,1,2048,64]{2,3,1,0:T(8,128)(2,1)}, bf16...) while((s32[]{:T(128)}, ...), condition=%wide.region_9.10_spmd.clone.clone, body=%wide.region_7.9_spmd.clone.sunk.clone | while | flops 2096110592 | bytes 198116496 | solution.py:215
  379.1 5.5 fusion.221
  384.6 7.4 fusion.217
  392.0 21.3 %fusion.220 = bf16[5,1,2048,64]{2,3,1,0:T(8,128)(2,1)} fusion(bf16[5,1,2048,64]{2,3,1,0:T(8,128)(2,1)} %get-tuple-element.438, s32[]{:T(128)S(6)} %copy.60, f32[3,512,2048]{2,1,0:T(8,128)} %fusion.217, f32[3,512,2048]{2,1,0:T(8,128)} %copy-done, f32[3,512]{1,0:T(4,128)S(1)} %dynamic-slice_bitcast_fusion.3, ...), kind=kOutput, calls=%fused_computation.45.clone.1.clone | convolution fusion | flops 437259776 | bytes 53167104 | tf_op jit(solution)/shard_map/while/body/eval_jaxpr/sgqk,sgqd->skd/dot_general | solution.py:210
  413.3 20.1 %fusion.219 = f32[5,1,3,512,64]{3,4,2,1,0:T(8,128)S(1)} fusion(f32[5,1,3,512,64]{3,4,2,1,0:T(8,128)S(1)} %get-tuple-element.437, s32[]{:T(128)S(6)} %copy.60, f32[3,512,2048]{2,1,0:T(8,128)} %fusion.217, f32[3,512,2048]{2,1,0:T(8,128)} %copy-done, f32[3,512]{1,0:T(4,128)S(1)} %dynamic-slice_bitcast_fusion.3, ...), kind=kOutput, calls=%fused_computation.47.clone.1.clone | convolution fusion | flops 437259776 | bytes 53101568 | tf_op jit(solution)/shard_map/while/body/eval_jaxpr/sgqk,skd->sgqd/dot_general | solution.py:207
  437.0 5.5 fusion.221
  442.6 7.4 fusion.217
  450.0 21.2 %fusion.220 = bf16[5,1,2048,64]{2,3,1,0:T(8,128)(2,1)} fusion(bf16[5,1,2048,64]{2,3,1,0:T(8,128)(2,1)} %get-tuple-element.438, s32[]{:T(128)S(6)} %copy.60, f32[3,512,2048]{2,1,0:T(8,128)} %fusion.217, f32[3,512,2048]{2,1,0:T(8,128)} %copy-done, f32[3,512]{1,0:T(4,128)S(1)} %dynamic-slice_bitcast_fusion.3, ...), kind=kOutput, calls=%fused_computation.45.clone.1.clone | convolution fusion | flops 437259776 | bytes 53167104 | tf_op jit(solution)/shard_map/while/body/eval_jaxpr/sgqk,sgqd->skd/dot_general | solution.py:210
  471.2 20.1 %fusion.219 = f32[5,1,3,512,64]{3,4,2,1,0:T(8,128)S(1)} fusion(f32[5,1,3,512,64]{3,4,2,1,0:T(8,128)S(1)} %get-tuple-element.437, s32[]{:T(128)S(6)} %copy.60, f32[3,512,2048]{2,1,0:T(8,128)} %fusion.217, f32[3,512,2048]{2,1,0:T(8,128)} %copy-done, f32[3,512]{1,0:T(4,128)S(1)} %dynamic-slice_bitcast_fusion.3, ...), kind=kOutput, calls=%fused_computation.47.clone.1.clone | convolution fusion | flops 437259776 | bytes 53101568 | tf_op jit(solution)/shard_map/while/body/eval_jaxpr/sgqk,skd->sgqd/dot_general | solution.py:207
  495.0 5.5 fusion.221
  500.5 7.4 fusion.217
  507.9 21.2 %fusion.220 = bf16[5,1,2048,64]{2,3,1,0:T(8,128)(2,1)} fusion(bf16[5,1,2048,64]{2,3,1,0:T(8,128)(2,1)} %get-tuple-element.438, s32[]{:T(128)S(6)} %copy.60, f32[3,512,2048]{2,1,0:T(8,128)} %fusion.217, f32[3,512,2048]{2,1,0:T(8,128)} %copy-done, f32[3,512]{1,0:T(4,128)S(1)} %dynamic-slice_bitcast_fusion.3, ...), kind=kOutput, calls=%fused_computation.45.clone.1.clone | convolution fusion | flops 437259776 | bytes 53167104 | tf_op jit(solution)/shard_map/while/body/eval_jaxpr/sgqk,sgqd->skd/dot_general | solution.py:210
  529.1 20.2 %fusion.219 = f32[5,1,3,512,64]{3,4,2,1,0:T(8,128)S(1)} fusion(f32[5,1,3,512,64]{3,4,2,1,0:T(8,128)S(1)} %get-tuple-element.437, s32[]{:T(128)S(6)} %copy.60, f32[3,512,2048]{2,1,0:T(8,128)} %fusion.217, f32[3,512,2048]{2,1,0:T(8,128)} %copy-done, f32[3,512]{1,0:T(4,128)S(1)} %dynamic-slice_bitcast_fusion.3, ...), kind=kOutput, calls=%fused_computation.47.clone.1.clone | convolution fusion | flops 437259776 | bytes 53101568 | tf_op jit(solution)/shard_map/while/body/eval_jaxpr/sgqk,skd->sgqd/dot_general | solution.py:207
  558.4 7.4 fusion.217
  565.8 21.2 %fusion.220 = bf16[5,1,2048,64]{2,3,1,0:T(8,128)(2,1)} fusion(bf16[5,1,2048,64]{2,3,1,0:T(8,128)(2,1)} %get-tuple-element.438, s32[]{:T(128)S(6)} %copy.60, f32[3,512,2048]{2,1,0:T(8,128)} %fusion.217, f32[3,512,2048]{2,1,0:T(8,128)} %copy-done, f32[3,512]{1,0:T(4,128)S(1)} %dynamic-slice_bitcast_fusion.3, ...), kind=kOutput, calls=%fused_computation.45.clone.1.clone | convolution fusion | flops 437259776 | bytes 53167104 | tf_op jit(solution)/shard_map/while/body/eval_jaxpr/sgqk,sgqd->skd/dot_general | solution.py:210
  587.1 20.1 %fusion.219 = f32[5,1,3,512,64]{3,4,2,1,0:T(8,128)S(1)} fusion(f32[5,1,3,512,64]{3,4,2,1,0:T(8,128)S(1)} %get-tuple-element.437, s32[]{:T(128)S(6)} %copy.60, f32[3,512,2048]{2,1,0:T(8,128)} %fusion.217, f32[3,512,2048]{2,1,0:T(8,128)} %copy-done, f32[3,512]{1,0:T(4,128)S(1)} %dynamic-slice_bitcast_fusion.3, ...), kind=kOutput, calls=%fused_computation.47.clone.1.clone | convolution fusion | flops 437259776 | bytes 53101568 | tf_op jit(solution)/shard_map/while/body/eval_jaxpr/sgqk,skd->sgqd/dot_general | solution.py:207
  610.8 5.5 fusion.221
  616.3 7.4 fusion.217
  623.8 21.2 %fusion.220 = bf16[5,1,2048,64]{2,3,1,0:T(8,128)(2,1)} fusion(bf16[5,1,2048,64]{2,3,1,0:T(8,128)(2,1)} %get-tuple-element.438, s32[]{:T(128)S(6)} %copy.60, f32[3,512,2048]{2,1,0:T(8,128)} %fusion.217, f32[3,512,2048]{2,1,0:T(8,128)} %copy-done, f32[3,512]{1,0:T(4,128)S(1)} %dynamic-slice_bitcast_fusion.3, ...), kind=kOutput, calls=%fused_computation.45.clone.1.clone | convolution fusion | flops 437259776 | bytes 53167104 | tf_op jit(solution)/shard_map/while/body/eval_jaxpr/sgqk,sgqd->skd/dot_general | solution.py:210
  645.0 20.1 %fusion.219 = f32[5,1,3,512,64]{3,4,2,1,0:T(8,128)S(1)} fusion(f32[5,1,3,512,64]{3,4,2,1,0:T(8,128)S(1)} %get-tuple-element.437, s32[]{:T(128)S(6)} %copy.60, f32[3,512,2048]{2,1,0:T(8,128)} %fusion.217, f32[3,512,2048]{2,1,0:T(8,128)} %copy-done, f32[3,512]{1,0:T(4,128)S(1)} %dynamic-slice_bitcast_fusion.3, ...), kind=kOutput, calls=%fused_computation.47.clone.1.clone | convolution fusion | flops 437259776 | bytes 53101568 | tf_op jit(solution)/shard_map/while/body/eval_jaxpr/sgqk,skd->sgqd/dot_general | solution.py:207
  674.9 24.7 %reduce-scatter.12.cloned.1.call-done = bf16[512,320]{0,1:T(8,128)(2,1)} async-done(((bf16[2048,320]{0,1:T(8,128)(2,1)}), bf16[512,320]{0,1:T(8,128)(2,1)}) %reduce-scatter.12.cloned.1.call-update) | async-done | bytes 327696 | tf_op jit(solution)/shard_map/reduce_scatter | solution.py:224
  702.3 30.1 %reduce-scatter.14.cloned.1.call-done = bf16[512,320]{0,1:T(8,128)(2,1)} async-done(((bf16[2048,320]{0,1:T(8,128)(2,1)}), bf16[512,320]{0,1:T(8,128)(2,1)}) %reduce-scatter.14.cloned.1.call-update) | async-done | bytes 327696 | tf_op jit(solution)/shard_map/reduce_scatter | solution.py:230
  734.9 7.0 convolution_convert_fusion
  741.9 7.9 copy.34
  757.4 6.2 convolution_convert_fusion.1
  763.6 6.1 convolution_convert_fusion.2
  770.4 22.2 %all-reduce.16.cloned.1.call-done = (bf16[960,320]{0,1:T(8,128)(2,1)}, bf16[960,320]{0,1:T(8,128)(2,1)}) async-done(((bf16[960,320]{0,1:T(8,128)(2,1)}, bf16[960,320]{0,1:T(8,128)(2,1)}), (bf16[960,320]{0,1:T(8,128)(2,1)}, bf16[960,320]{0,1:T(8,128)(2,1)})) %all-reduce.16.cloned.1.call-update) | async-done | bytes 1228816
  794.5 62.5 %reduce-scatter.24.cloned.1.call-done = bf16[640,960]{1,0:T(8,128)(2,1)} async-done(((bf16[2560,960]{1,0:T(8,128)(2,1)}), bf16[640,960]{1,0:T(8,128)(2,1)}) %reduce-scatter.24.cloned.1.call-update) | async-done | bytes 1228816
  859.7 35.0 %reduce-scatter.16.cloned.1.call-done = bf16[240,960]{1,0:T(8,128)(2,1)} async-done(((bf16[960,960]{1,0:T(8,128)(2,1)}), bf16[240,960]{1,0:T(8,128)(2,1)}) %reduce-scatter.16.cloned.1.call-update) | async-done | bytes 460816 | tf_op jit(solution)/shard_map/reduce_scatter | solution.py:258
  894.7 37.8 %reduce-scatter.18.cloned.1.call-done = bf16[240,960]{1,0:T(8,128)(2,1)} async-done(((bf16[960,960]{1,0:T(8,128)(2,1)}), bf16[240,960]{1,0:T(8,128)(2,1)}) %reduce-scatter.18.cloned.1.call-update) | async-done | bytes 460816 | tf_op jit(solution)/shard_map/reduce_scatter | solution.py:267
  932.4 61.6 %reduce-scatter.22.cloned.1.call-done = bf16[240,2560]{1,0:T(8,128)(2,1)} async-done(((bf16[960,2560]{1,0:T(8,128)(2,1)}), bf16[240,2560]{1,0:T(8,128)(2,1)}) %reduce-scatter.22.cloned.1.call-update) | async-done | bytes 1228816 | tf_op jit(solution)/shard_map/reduce_scatter | solution.py:273
  994.1 61.6 %reduce-scatter.20.cloned.1.call-done = bf16[240,2560]{1,0:T(8,128)(2,1)} async-done(((bf16[960,2560]{1,0:T(8,128)(2,1)}), bf16[240,2560]{1,0:T(8,128)(2,1)}) %reduce-scatter.20.cloned.1.call-update) | async-done | bytes 1228816 | tf_op jit(solution)/shard_map/reduce_scatter | solution.py:270
  1058.6 6.2 add_convert_fusion
  1067.2 9.1 all-reduce.8
  1076.5 15.5 %all-reduce.6 = (bf16[240]{0:T(256)(128)(2,1)S(1)}, bf16[240]{0:T(256)(128)(2,1)S(1)}) all-reduce(bf16[240]{0:T(256)(128)(2,1)S(1)} %dynamic-slice.7, bf16[240]{0:T(256)(128)(2,1)S(1)} %dynamic-slice.9), channel_id=1, replica_groups=mesh['fsdp'=4,'dp'=8] {'dp'}, use_global_device_ids=true, to_apply=%region_29.30 | all-reduce | flops 480 | bytes 1920 | tf_op jit(solution)/shard_map/psum | solution.py:294
  1096.5 77.4 %all-reduce.14.cloned.1.call-done = (bf16[240,960]{1,0:T(8,128)(2,1)}, bf16[240,320]{0,1:T(8,128)(2,1)}, bf16[240,320]{0,1:T(8,128)(2,1)}, bf16[240,960]{1,0:T(8...) async-done(((bf16[240,960]{1,0:T(8,128)(2,1)}, bf16[240,320]{0,1:T(8,128)(2,1)}, bf16[240,320]{0,1:T(8,128)(2,1)}, ...) | async-done | bytes 4915216 | tf_op jit(solution)/shard_map/psum | solution.py:287
  (222 shorter events, 120.2 us)
Async XLA Ops:
  7.2 29.6 %copy-start.3 = (bf16[512,960]{0,1:T(8,128)(2,1)S(1)}, bf16[512,960]{0,1:T(8,128)(2,1)}, u32[]{:S(2)}) copy-start(bf16[512,960]{0,1:T(8,128)(2,1)} %param.16) | copy-start | bytes 2949124
  7.2 28.5 %copy-start.34 = (s32[1,8]{1,0:T(1,128)S(1)}, s32[1,8]{1,0:T(1,128)}, u32[]{:S(2)}) copy-start(s32[1,8]{1,0:T(1,128)} %param.17) | copy-start | bytes 100
  7.2 60.2 %all-gather.12.cloned.1.call-start = ((), (), s32[]{:S(2)}) async-start(), calls=%async_computation.8 | async-start | bytes 1638400 | tf_op jit(solution)/shard_map/all_gather | solution.py:127
  8.8 125.8 %copy-start.30 = (f32[512]{0:T(512)}, f32[512]{0:T(512)S(1)}, u32[]{:S(2)}) copy-start(f32[512]{0:T(512)S(1)} %add_rsqrt_fusion.1) | copy-start | bytes 6148
  23.8 110.7 %copy-start.28 = (f32[960]{0:T(1024)}, f32[960]{0:T(1024)S(1)}, u32[]{:S(2)}) copy-start(f32[960]{0:T(1024)S(1)} %convert_element_type.188) | copy-start | bytes 11524
  35.7 2.6 copy-start.13
  36.8 100.7 %copy-start.16 = (f32[512,32]{0,1:T(8,128)}, f32[512,32]{0,1:T(8,128)S(1)}, u32[]{:S(2)}) copy-start(f32[512,32]{0,1:T(8,128)S(1)} %get-tuple-element.228) | copy-start | bytes 196612
  36.8 1.5 copy-start.27
  38.3 60.2 %all-gather.14.cloned.1.call-start = ((), (), s32[]{:S(2)}) async-start(), calls=%async_computation.9 | async-start | bytes 1638400 | tf_op jit(solution)/shard_map/all_gather | solution.py:128
  49.6 3.3 copy-start.11
  50.9 83.7 %all-gather.10.cloned.1.call-start = ((), (), s32[]{:S(2)}) async-start(), calls=%async_computation.7 | async-start | bytes 2457600 | tf_op jit(solution)/shard_map/all_gather | solution.py:83
  51.7 190.5 %all-gather.16.cloned.1.call-start = ((), (), s32[]{:S(2)}) async-start(), calls=%async_computation.10 | async-start | bytes 2457600 | tf_op jit(solution)/shard_map/all_gather | solution.py:86
  52.2 194.7 %all-gather.20.cloned.1.call-start = ((), (), s32[]{:S(2)}) async-start(), calls=%async_computation.12 | async-start | bytes 6144000 | tf_op jit(solution)/shard_map/all_gather | solution.py:88
  52.8 238.6 %all-gather.18.cloned.1.call-start = ((), (), s32[]{:S(2)}) async-start(), calls=%async_computation.11 | async-start | bytes 6144000 | tf_op jit(solution)/shard_map/all_gather | solution.py:87
  53.4 298.6 %all-gather.22.cloned.1.call-start = ((), (), s32[]{:S(2)}) async-start(), calls=%async_computation.13 | async-start | bytes 6144000 | tf_op jit(solution)/shard_map/all_gather | solution.py:89
  54.2 645.4 %reduce-scatter.12.cloned.1.call-start = ((), (), s32[]{:S(2)}) async-start(), calls=%async_computation.14 | async-start | bytes 1638400 | tf_op jit(solution)/shard_map/reduce_scatter | solution.py:224
  242.1 1.1 copy-start.9
  242.1 1.4 copy-start.10
  246.6 124.7 %copy-start.5 = (f32[512,960]{0,1:T(8,128)}, f32[512,960]{0,1:T(8,128)S(1)}, u32[]{:S(2)}) copy-start(f32[512,960]{0,1:T(8,128)S(1)} %get-tuple-element.232) | copy-start | bytes 5898244
  246.9 44.6 %copy-start.1 = (bf16[512,960]{0,1:T(8,128)(2,1)}, bf16[512,960]{0,1:T(8,128)(2,1)S(1)}, u32[]{:S(2)}) copy-start(bf16[512,960]{0,1:T(8,128)(2,1)S(1)} %multiply_convert_fusion.4) | copy-start | bytes 2949124
  352.0 10.5 copy-start.8
  362.5 2.7 copy-start.36
  362.5 2.7 copy-start.37
  365.2 6.1 copy-start.23
  371.4 1.5 copy-start.33
  372.9 2.2 copy-start.7
  372.9 2.4 copy-start.15
  379.1 5.5 copy-start
  437.0 5.6 copy-start
  494.9 5.5 copy-start
  552.9 5.5 copy-start
  610.8 5.6 copy-start
  670.0 62.4 %reduce-scatter.14.cloned.1.call-start = ((), (), s32[]{:S(2)}) async-start(), calls=%async_computation.15 | async-start | bytes 1638400 | tf_op jit(solution)/shard_map/reduce_scatter | solution.py:230
  673.3 27.3 %copy-start.17 = (f32[512,32]{0,1:T(8,128)S(1)}, f32[512,32]{0,1:T(8,128)}, u32[]{:S(2)}) copy-start(f32[512,32]{0,1:T(8,128)} %copy-done.16) | copy-start | bytes 196612
  673.3 27.3 %copy-start.24 = (f32[512,32]{0,1:T(8,128)S(1)}, f32[512,32]{0,1:T(8,128)}, u32[]{:S(2)}) copy-start(f32[512,32]{0,1:T(8,128)} %get-tuple-element.226) | copy-start | bytes 196612
  674.8 26.0 %copy-start.4 = (bf16[512,960]{0,1:T(8,128)(2,1)S(1)}, bf16[512,960]{0,1:T(8,128)(2,1)}, u32[]{:S(2)}) copy-start(bf16[512,960]{0,1:T(8,128)(2,1)} %param.16) | copy-start | bytes 2949124
  674.8 26.0 %copy-start.29 = (f32[960]{0:T(1024)S(1)}, f32[960]{0:T(1024)}, u32[]{:S(2)}) copy-start(f32[960]{0:T(1024)} %copy-done.28) | copy-start | bytes 11524
  674.8 26.0 %copy-start.31 = (f32[512]{0:T(512)S(1)}, f32[512]{0:T(512)}, u32[]{:S(2)}) copy-start(f32[512]{0:T(512)} %copy-done.30) | copy-start | bytes 6148
  674.8 117.8 %all-reduce.16.cloned.1.call-start = ((), (), s32[]{:S(2)}) async-start(), calls=%async_computation.22 | async-start | bytes 2621440
  700.7 34.1 %copy-start.18 = (bf16[512,5,64]{0,2,1:T(8,128)(2,1)}, bf16[512,5,64]{0,2,1:T(8,128)(2,1)S(1)}, u32[]{:S(2)}) copy-start(bf16[512,5,64]{0,2,1:T(8,128)(2,1)S(1)} %pad_maximum_fusion.2) | copy-start | bytes 983044
  734.9 122.2 %reduce-scatter.24.cloned.1.call-start = ((), (), s32[]{:S(2)}) async-start(), calls=%async_computation.20 | async-start | bytes 6553600
  749.9 144.8 %reduce-scatter.16.cloned.1.call-start = ((), (), s32[]{:S(2)}) async-start(), calls=%async_computation.16 | async-start | bytes 2457600 | tf_op jit(solution)/shard_map/reduce_scatter | solution.py:258
  752.8 4.5 copy-start.2
  752.8 179.6 %reduce-scatter.18.cloned.1.call-start = ((), (), s32[]{:S(2)}) async-start(), calls=%async_computation.17 | async-start | bytes 2457600 | tf_op jit(solution)/shard_map/reduce_scatter | solution.py:267
  757.3 236.7 %reduce-scatter.22.cloned.1.call-start = ((), (), s32[]{:S(2)}) async-start(), calls=%async_computation.19 | async-start | bytes 6144000 | tf_op jit(solution)/shard_map/reduce_scatter | solution.py:273
  763.6 292.1 %reduce-scatter.20.cloned.1.call-start = ((), (), s32[]{:S(2)}) async-start(), calls=%async_computation.18 | async-start | bytes 6144000 | tf_op jit(solution)/shard_map/reduce_scatter | solution.py:270
  769.7 404.2 %all-reduce.14.cloned.1.call-start = ((), (), s32[]{:S(2)}) async-start(), calls=%async_computation.21 | async-start | bytes 9994240 | tf_op jit(solution)/shard_map/psum | solution.py:287
  1055.7 2.9 copy-start.6
  1055.7 2.9 copy-start.35
  1058.6 6.2 copy-start.14
  1058.6 6.2 copy-start.19
  1064.8 1.1 copy-start.12
  1064.8 1.2 copy-start.26
  1066.0 1.2 copy-start.32
  1173.9 5.5 copy-start.25
  1173.9 6.6 copy-start.22
  1179.4 2.8 copy-start.21
  1182.2 1.7 copy-start.20
Sparse Core Ops, SparseCore 0:
  38.4 28.9 all-gather.11
  69.8 28.6 all-gather.13
  100.3 34.2 all-gather.9
  136.3 34.2 all-gather.15
  172.2 58.6 all-gather.19
  232.7 58.7 all-gather.17
  293.3 58.6 all-gather.21
  670.2 29.3 reduce-scatter.11
  703.0 29.3 reduce-scatter.13
  735.9 56.6 all-reduce.15
  795.6 61.4 reduce-scatter.23
  860.5 34.0 reduce-scatter.15
  898.3 34.0 reduce-scatter.17
  935.3 58.7 reduce-scatter.21
  996.9 58.7 reduce-scatter.19
  1059.1 114.7 all-reduce.13
where the time goes:
time: 1200 us; the launch traced here: 1190 us
  waiting for transfers between devices  570 us (48%)
  matrix products  438 us (36%)
  other arithmetic  63.7 us (5%)
  blocking collectives  56.9 us (5%)
  local copies, waits for them, and re-layouts  45.8 us (4%)
  between operations  16.2 us (1%)
    dot_general x5, matrix products, backward_head(): jnp.einsum('sgqk,sgqd->skd', grad_scores, query, preferred_element_type=j...  106 us
    dot_general x5, matrix products, backward_head(): jnp.einsum('sgqk,skd->sgqd', grad_scores, keys, preferred_element_type=jn...  101 us
    unnamed x18, waiting for transfers between devices  87.8 us
    psum x1, waiting for transfers between devices, on_device(): lax.psum(owned[0].astype(jnp.bfloat16), 'dp').astype(jnp.float32)  77.4 us
    reduce_scatter x1, waiting for transfers between devices, on_device(): lax.psum_scatter(grad_w_up.astype(jnp.bfloat16), 'fsdp', scatter_dimensio...  61.6 us
    reduce_scatter x1, waiting for transfers between devices, on_device(): lax.psum_scatter(grad_w_gate.astype(jnp.bfloat16), 'fsdp', scatter_dimens...  61.6 us
    all_gather x1, waiting for transfers between devices, on_device(): lax.all_gather(w_down, 'fsdp', axis=0, tiled=True)  53.5 us
    reduce_scatter x1, waiting for transfers between devices, on_device(): lax.psum_scatter(grad_w_out.astype(jnp.bfloat16), 'fsdp', scatter_dimensi...  37.8 us
  transfers between devices with their start and end apart: 16, of which 14 were waited for; matrix products, arithmetic and copies ran while one was open for 17% of the time, Pallas kernels for 0%

commit v1 on v0

v1 whole, which is shorter than its diff:
```python
import functools
import jax
import jax.numpy as jnp
from jax import lax
from jax.experimental import pallas as pl
from jax.experimental.pallas import tpu as pltpu
from jax.sharding import PartitionSpec as P

HEADS = 15
KV_HEADS = 5
HEAD_DIM = 64
NEG = -1e30


def product(left, right, contract):
    return lax.dot_general(
        left, right, (contract, ((), ())), preferred_element_type=jnp.float32
    )


ROW_ROW = ((1,), (1,))
PLAIN = ((1,), (0,))


def attend_kernel(tile, query_ref, key_ref, value_t_ref, qplace_ref, kplace_ref, out_ref, lse_ref):
    keys = key_ref[0, 0]
    values_t = value_t_ref[0, 0]
    kplace = kplace_ref[0]

    @pl.loop(0, query_ref.shape[2] // tile)
    def _(step):
        rows = pl.ds(pl.multiple_of(step * tile, tile), tile)
        query = query_ref[0, 0, rows]
        scores = product(keys, query, ROW_ROW)
        allowed = kplace <= qplace_ref[0, step]
        scores = jnp.where(allowed, scores, NEG)
        top = jnp.max(scores, axis=0, keepdims=True)
        powers = jnp.exp(scores - top)
        total = jnp.sum(powers, axis=0, keepdims=True)
        mixed = product(values_t, powers.astype(jnp.bfloat16), PLAIN) / total
        out_ref[0, 0, rows] = mixed.T.astype(jnp.bfloat16)
        lse_ref[0, 0, step] = top + jnp.log(total)


def attend_back_kernel(
    tile,
    query_ref,
    key_ref,
    key_t_ref,
    value_ref,
    grad_ref,
    lse_ref,
    qplace_ref,
    kplace_ref,
    dq_ref,
    dk_ref,
    dv_ref,
):
    keys = key_ref[0, 0]
    keys_t = key_t_ref[0, 0]
    values = value_ref[0, 0]
    kplace = kplace_ref[0]
    dk_ref[...] = jnp.zeros_like(dk_ref)
    dv_ref[...] = jnp.zeros_like(dv_ref)

    @pl.loop(0, query_ref.shape[2] // tile)
    def _(step):
        rows = pl.ds(pl.multiple_of(step * tile, tile), tile)
        query = query_ref[0, 0, rows]
        grad = grad_ref[0, 0, rows]
        scores = product(keys, query, ROW_ROW)
        allowed = kplace <= qplace_ref[0, step]
        probs = jnp.exp(jnp.where(allowed, scores, NEG) - lse_ref[0, 0, step])
        dv_ref[0, 0] += product(probs.astype(jnp.bfloat16), grad, PLAIN)
        dprobs = product(values, grad, ROW_ROW)
        centre = jnp.sum(probs * dprobs, axis=0, keepdims=True)
        dscores = (probs * (dprobs - centre)).astype(jnp.bfloat16)
        dk_ref[0, 0] += product(dscores, query, PLAIN)
        dq_ref[0, 0, rows] = product(keys_t, dscores, PLAIN).T * HEAD_DIM**-0.5


def block(shape):
    return pl.BlockSpec((1, 1) + shape, lambda h, s: (h, s) + (0,) * len(shape))


def by_seq(shape):
    return pl.BlockSpec((1,) + shape, lambda h, s: (s,) + (0,) * len(shape))


def attend(query, keys, values_t, qplace, kplace):
    heads, seqs, rows, dim = query.shape
    length = keys.shape[2]
    tiles, tile = qplace.shape[1], qplace.shape[3]
    return pl.pallas_call(
        functools.partial(attend_kernel, tile),
        grid=(heads, seqs),
        in_specs=[
            block((rows, dim)),
            block((length, dim)),
            block((dim, length)),
            by_seq((tiles, 1, tile)),
            by_seq((length, 1)),
        ],
        out_specs=[block((rows, dim)), block((tiles, 1, tile))],
        out_shape=[
            jax.ShapeDtypeStruct((heads, seqs, rows, dim), jnp.bfloat16),
            jax.ShapeDtypeStruct((heads, seqs, tiles, 1, tile), jnp.float32),
        ],
        cost_estimate=pl.CostEstimate(
            flops=16 * heads * seqs * rows * length * dim,
            bytes_accessed=4 * heads * seqs * (rows + length) * dim * 2,
            transcendentals=heads * seqs * rows * length,
        ),
        compiler_params=pltpu.CompilerParams(vmem_limit_bytes=40 * 2**20),
        name="attend",
    )(query, keys, values_t, qplace, kplace)


def attend_back(query, keys, keys_t, values, grad, lse, qplace, kplace):
    heads, seqs, rows, dim = query.shape
    length = keys.shape[2]
    tiles, tile = qplace.shape[1], qplace.shape[3]
    return pl.pallas_call(
        functools.partial(attend_back_kernel, tile),
        grid=(heads, seqs),
        in_specs=[
            block((rows, dim)),
            block((length, dim)),
            block((dim, length)),
            block((length, dim)),
            block((rows, dim)),
            block((tiles, 1, tile)),
            by_seq((tiles, 1, tile)),
            by_seq((length, 1)),
        ],
        out_specs=[block((rows, dim)), block((length, dim)), block((length, dim))],
        out_shape=[
            jax.ShapeDtypeStruct((heads, seqs, rows, dim), jnp.float32),
            jax.ShapeDtypeStruct((heads, seqs, length, dim), jnp.float32),
            jax.ShapeDtypeStruct((heads, seqs, length, dim), jnp.float32),
        ],
        cost_estimate=pl.CostEstimate(
            flops=40 * heads * seqs * rows * length * dim,
            bytes_accessed=4 * heads * seqs * (rows + length) * dim * 4,
            transcendentals=heads * seqs * rows * length,
        ),
        compiler_params=pltpu.CompilerParams(vmem_limit_bytes=48 * 2**20),
        name="attend_back",
    )(query, keys, keys_t, values, grad, lse, qplace, kplace)


epsilon = 1e-05
rope_base = 100000.0
ROWS = ("fsdp", "dz", "core")


def rope_tables(places, head_dim):
    half_dim = head_dim // 2
    rates = rope_base ** (-2.0 * jnp.arange(half_dim, dtype=jnp.float32) / head_dim)
    angles = places.astype(jnp.float32)[:, None] * rates[None, :]
    return (jnp.cos(angles)[:, None, :], jnp.sin(angles)[:, None, :])


def rotate(field, cosine, sine_part):
    half_dim = field.shape[-1] // 2
    first = field[..., :half_dim]
    second = field[..., half_dim:]
    return jnp.concatenate(
        [first * cosine - second * sine_part, second * cosine + first * sine_part], axis=-1
    )


def rms_scale(values):
    return lax.rsqrt(jnp.mean(values * values, axis=-1, keepdims=True) + epsilon)


def norm_back(grad_normed, values, scale_rows, gain):
    scaled = values * scale_rows
    weighted = grad_normed * gain
    grad_values = scale_rows * (
        weighted - scaled * jnp.mean(weighted * scaled, axis=-1, keepdims=True)
    )
    return (grad_values, jnp.sum(grad_normed * scaled, axis=0))


def ein(spec, left, right):
    return jnp.einsum(spec, left, right, preferred_element_type=jnp.float32)


def gather(shard, axes):
    return lax.all_gather(shard, axes, axis=0, tiled=True)


def scatter(field, axes):
    return lax.psum_scatter(field, axes, scatter_dimension=0, tiled=True)


def both_cores(part):
    other = lax.ppermute(part, "core", [(0, 1), (1, 0)])
    first_core = lax.axis_index("core") == 0
    return (
        jnp.where(first_core, part, other).astype(jnp.float32),
        jnp.where(first_core, other, part).astype(jnp.float32),
    )


def on_device(
    tokens,
    span_table,
    w_query,
    w_key,
    w_value,
    w_out,
    w_gate,
    w_up,
    w_down,
    gain_attn,
    gain_ffn,
    cotangent,
):
    bf16 = jnp.bfloat16
    groups = lax.axis_size("fsdp")
    index = lax.axis_index("fsdp")
    core = lax.axis_index("core")
    first_core = core == 0
    rows, width = tokens.shape
    seqs = span_table.shape[0]
    span = rows // (2 * seqs)
    per_kv = HEADS // KV_HEADS
    length = groups * 2 * span
    kv_width = w_key.shape[1]
    qkv_width = width + 2 * kv_width
    half = qkv_width // 2

    projections = jnp.concatenate([w_query, w_key, w_value], axis=1)
    early = jnp.concatenate(
        [
            jnp.where(first_core, projections[:, :half], projections[:, half:]),
            jnp.where(first_core, gain_attn, gain_ffn)[:, None],
        ],
        axis=1,
    )
    early_full = gather(early, ("core", "fsdp")).reshape(2, width, half + 1)
    qkv_full = early_full[:, :, :half]
    gains = early_full[:, :, half].astype(jnp.float32)
    attn_gain, ffn_gain = gains[0], gains[1]
    half_out = width // 2
    out_full = gather(
        jnp.where(first_core, w_out[:, :half_out], w_out[:, half_out:]), ("core", "fsdp")
    ).reshape(2, width, half_out)
    ffn_full = gather(jnp.where(first_core, w_gate, w_up), ("core", "fsdp")).reshape(
        2, width, w_gate.shape[1]
    )
    half_down = w_down.shape[0] // 2
    down_full = gather(
        jnp.where(first_core, w_down[:half_down], w_down[half_down:]), ("fsdp", "core")
    )

    offsets = jnp.arange(span, dtype=jnp.int32)
    mine = lax.dynamic_slice_in_dim(span_table, 2 * index, 2, 1)
    query_place = (mine[:, :, None] * span + offsets).reshape(seqs, 2 * span)
    key_place = (span_table[:, :, None] * span + offsets).reshape(seqs, length, 1)
    tile_place = jnp.broadcast_to(
        query_place.reshape(seqs, 1, 2, 1, span), (seqs, per_kv, 2, 1, span)
    ).reshape(seqs, per_kv * 2, 1, span)
    cosine, sine_part = rope_tables(query_place.reshape(-1), HEAD_DIM)
    inputs = tokens.astype(jnp.float32)
    scale_one = rms_scale(inputs)
    normed_one = (inputs * scale_one * attn_gain).astype(bf16)
    halves = ein("rd,bde->bre", normed_one, qkv_full)
    qkv = jnp.concatenate([halves[0], halves[1]], axis=1)
    query_rows = rotate(
        qkv[:, :width].reshape(rows, HEADS, HEAD_DIM), cosine, sine_part
    ).astype(bf16) * jnp.asarray(HEAD_DIM**-0.5, bf16)
    key_rows = rotate(
        qkv[:, width : width + kv_width].reshape(rows, KV_HEADS, HEAD_DIM), cosine, sine_part
    ).astype(bf16)
    key_value = jnp.concatenate(
        [key_rows.reshape(rows, kv_width), qkv[:, width + kv_width :].astype(bf16)], axis=1
    )
    spread = gather(key_value, "fsdp").reshape(
        groups, seqs, 2 * span, 2, KV_HEADS, HEAD_DIM
    )
    key_value_heads = spread.transpose(3, 4, 1, 0, 2, 5).reshape(
        2, KV_HEADS, seqs, length, HEAD_DIM
    )
    keys, values = key_value_heads[0], key_value_heads[1]
    turned = spread.transpose(3, 4, 1, 5, 0, 2).reshape(2, KV_HEADS, seqs, HEAD_DIM, length)
    keys_t, values_t = turned[0], turned[1]

    def to_heads(field):
        return (
            field.reshape(seqs, 2 * span, KV_HEADS, per_kv, HEAD_DIM)
            .transpose(2, 0, 3, 1, 4)
            .reshape(KV_HEADS, seqs, per_kv * 2 * span, HEAD_DIM)
        )

    def from_heads(field):
        return (
            field.reshape(KV_HEADS, seqs, per_kv, 2 * span, HEAD_DIM)
            .transpose(1, 3, 0, 2, 4)
            .reshape(rows, HEADS * HEAD_DIM)
        )

    query_heads = to_heads(query_rows)
    mixed_heads, log_sums = attend(query_heads, keys, values_t, tile_place, key_place)
    attended = from_heads(mixed_heads)
    hidden = inputs + ein("rd,bde->rbe", attended, out_full).reshape(rows, width)
    scale_two = rms_scale(hidden)
    normed_two = (hidden * scale_two * ffn_gain).astype(bf16)
    both = ein("rd,bde->bre", normed_two, ffn_full)
    gate, upward = both[0], both[1]
    sigma = jax.nn.sigmoid(gate)
    activated = gate * sigma
    inner = (activated * upward).astype(bf16)
    output = (hidden + ein("re,ed->rd", inner, down_full)).astype(bf16)

    grad_out = cotangent.astype(jnp.float32)
    grad_down = ein("re,rd->ed", inner, cotangent).astype(bf16)
    grad_inner = ein("rd,ed->re", cotangent, down_full)
    grad_gate = (grad_inner * upward * sigma * (1.0 + gate * (1.0 - sigma))).astype(bf16)
    grad_up = (grad_inner * activated).astype(bf16)
    grad_both = jnp.stack([grad_gate, grad_up])
    grad_ffn = ein("rd,bre->bde", normed_two, grad_both).astype(bf16).reshape(2 * width, -1)
    grad_normed_two = ein("bre,bde->rd", grad_both, ffn_full)
    grad_hidden_norm, grad_gain_ffn = norm_back(grad_normed_two, hidden, scale_two, ffn_gain)
    grad_hidden = grad_out + grad_hidden_norm
    grad_branch = grad_hidden.astype(bf16)
    branch_halves = grad_branch.reshape(rows, 2, half_out)
    grad_proj = ein("rd,rbe->bde", attended, branch_halves).astype(bf16).reshape(2 * width, -1)
    grad_attended = ein("rbe,bde->rd", branch_halves, out_full).astype(bf16)
    grad_attended, grad_down, grad_ffn, grad_proj = lax.optimization_barrier(
        (grad_attended, grad_down, grad_ffn, grad_proj)
    )
    down_part = scatter(grad_down, ("fsdp", "core"))
    ffn_part = scatter(grad_ffn, ("core", "fsdp"))
    out_part = scatter(grad_proj, ("core", "fsdp"))
    grad_query_heads, grad_key_heads, grad_value_heads = attend_back(
        query_heads,
        keys,
        keys_t,
        values,
        to_heads(grad_attended),
        log_sums,
        tile_place,
        key_place,
    )
    grad_spread = (
        jnp.stack([grad_key_heads, grad_value_heads])
        .astype(bf16)
        .reshape(2, KV_HEADS, seqs, groups, 2 * span, HEAD_DIM)
        .transpose(3, 2, 4, 0, 1, 5)
        .reshape(groups * rows, 2 * kv_width)
    )
    grad_spread, down_part, ffn_part, out_part = lax.optimization_barrier(
        (grad_spread, down_part, ffn_part, out_part)
    )
    grad_key_value = scatter(grad_spread, "fsdp")
    grad_key_rows = rotate(
        grad_key_value[:, :kv_width].astype(jnp.float32).reshape(rows, KV_HEADS, HEAD_DIM),
        cosine,
        -sine_part,
    )
    grad_query_rows = rotate(
        from_heads(grad_query_heads).reshape(rows, HEADS, HEAD_DIM), cosine, -sine_part
    )
    grad_qkv = jnp.concatenate(
        [
            grad_query_rows.reshape(rows, width).astype(bf16),
            grad_key_rows.reshape(rows, kv_width).astype(bf16),
            grad_key_value[:, kv_width:],
        ],
        axis=1,
    )
    grad_halves = jnp.stack([grad_qkv[:, :half], grad_qkv[:, half:]])
    grad_normed_one = ein("bre,bde->rd", grad_halves, qkv_full)
    grad_input_norm, grad_gain_attn = norm_back(grad_normed_one, inputs, scale_one, attn_gain)
    grad_tokens = grad_hidden + grad_input_norm
    grad_gains = jnp.stack([grad_gain_attn, grad_gain_ffn])[:, :, None]
    grad_early = (
        jnp.concatenate([ein("rd,bre->bde", normed_one, grad_halves), grad_gains], axis=2)
        .astype(bf16)
        .reshape(2 * width, half + 1)
    )
    sums = lax.psum((down_part, ffn_part, out_part), "dz")
    grad_early, down_sum, ffn_sum, out_sum = lax.optimization_barrier((grad_early,) + tuple(sums))
    early_part = scatter(grad_early, ("core", "fsdp"))
    early_sum = lax.psum(early_part, "dz")

    down_both = jnp.concatenate(both_cores(down_sum), axis=0)
    ffn_both = both_cores(ffn_sum)
    out_both = both_cores(out_sum)
    early_both = both_cores(early_sum)
    grad_projections = jnp.concatenate([early_both[0][:, :half], early_both[1][:, :half]], axis=1)
    return (
        output,
        grad_tokens,
        grad_projections[:, :width],
        grad_projections[:, width : width + kv_width],
        grad_projections[:, width + kv_width :],
        jnp.concatenate([out_both[0], out_both[1]], axis=1),
        ffn_both[0],
        ffn_both[1],
        down_both,
        early_both[0][:, half],
        early_both[1][:, half],
    )


def solution(mesh):
    fsdp = mesh.shape["fsdp"]
    split = jax.sharding.Mesh(mesh.devices.reshape(fsdp, -1, 2), ROWS)
    weight = P("fsdp", None)
    row = P(ROWS, None)
    return jax.shard_map(
        on_device,
        mesh=split,
        in_specs=(row, P(("dz", "core"), None)) + (weight,) * 7 + (P("fsdp"),) * 2 + (row,),
        out_specs=(row, row) + (weight,) * 7 + (P("fsdp"),) * 2,
        check_vma=False,
    )
```

time: 1200 us -> 700 us (0.58)
  matrix products: 438 us -> 65.8 us
  waiting for transfers between devices: 570 us -> 355 us
  Pallas kernels: 0 us -> 108 us
  local copies, waits for them, and re-layouts: 45.8 us -> 113 us
  blocking collectives: 56.9 us -> 0 us
  other arithmetic: 63.7 us -> 34.9 us
    dot_general x56 -> x12, matrix products: 438 us -> 65.8 us  [ein(): return jnp.einsum(spec, left, right, preferred_element_type=jnp.float32)]
    reduce_scatter x6 -> x3, waiting for transfers between devices: 251 us -> 117 us  [scatter(): return lax.psum_scatter(field, axes, scatter_dimension=0, tiled=True)]
    pallas_call x0 -> x2, Pallas kernels: none -> 108 us  [the longest x1 68.4 us: attend_back(): pl.pallas_call(functools.partial(attend_back_kernel, tile), grid=(heads,...]
    all_gather x7 -> x5, waiting for transfers between devices: 154 us -> 95.8 us  [gather(): return lax.all_gather(shard, axes, axis=0, tiled=True)]
    unnamed x18 -> x14, waiting for transfers between devices: 87.8 us -> 36.5 us
    reduce_sum x5 -> x0, other arithmetic: 33.8 us -> none  [forward_head(): totals = jnp.sum(powers, axis=-1, keepdims=True)]
    psum x1 -> x2, waiting for transfers between devices: 77.4 us -> 105 us  [the longest x1 71.2 us: on_device(): sums = lax.psum((down_part, ffn_part, out_part), 'dz')]
    slice x0 -> x13, local copies, waits for them, and re-layouts: none -> 21.6 us  [the longest x1 7.53 us: rotate(): second = field[..., half_dim:]]
  transfers between devices with their start and end apart: 16 -> 16, of which waited for: 14 -> 10; matrix products, arithmetic and copies ran while one was open for 17% -> 21% of each run, Pallas kernels for 0% -> 16%
where the time goes in v1:
time: 700 us; the launch traced here: 694 us
  waiting for transfers between devices  355 us (51%)
  local copies, waits for them, and re-layouts  113 us (16%)
  Pallas kernels  108 us (15%)
  matrix products  65.8 us (9%)
  other arithmetic  34.9 us (5%)
  between operations  15.1 us (2%)
    reduce_scatter x3, waiting for transfers between devices, scatter(): return lax.psum_scatter(field, axes, scatter_dimension=0, tiled=True)  117 us
    all_gather x5, waiting for transfers between devices, gather(): return lax.all_gather(shard, axes, axis=0, tiled=True)  95.8 us
    psum x1, waiting for transfers between devices, on_device(): sums = lax.psum((down_part, ffn_part, out_part), 'dz')  71.2 us
    pallas_call x1, Pallas kernels, attend_back(): pl.pallas_call(functools.partial(attend_back_kernel, tile), grid=(heads,...  68.4 us
    dot_general x12, matrix products, ein(): return jnp.einsum(spec, left, right, preferred_element_type=jnp.float32)  65.8 us
    unnamed x85, local copies, waits for them, and re-layouts  40 us
    pallas_call x1, Pallas kernels, attend(): pl.pallas_call(functools.partial(attend_kernel, tile), grid=(heads, seqs)...  39.5 us
    unnamed x14, waiting for transfers between devices  36.5 us
  transfers between devices with their start and end apart: 16, of which 10 were waited for; matrix products, arithmetic and copies ran while one was open for 21% of the time, Pallas kernels for 16%

profile of v1, /device:TPU:0, one launch (start us, length us, event | category | flops | bytes accessed | tf_op | source)
XLA Modules:
  0.0 693.5 jit_solution(8271170704446281315)
XLA Ops:
  8.0 1.2 copy.104
  13.7 33.4 %all-gather.15.cloned.1.call-done = bf16[8,240,801]{1,2,0:T(8,128)(2,1)} async-done(((bf16[1,240,801]{1,2,0:T(8,128)(2,1)}), bf16[8,240,801]{1,2,0:T(8,128)(2,1)}) %all-gather.15.cloned.1.call-update) | async-done | bytes 3075856 | tf_op jit(solution)/shard_map/all_gather | solution.py:191
  47.1 6.0 copy.106
  55.1 2.0 fusion.24
  59.4 2.5 broadcast_select_fusion
  61.9 2.8 fusion.44
  64.7 2.2 copy.137
  66.9 2.2 copy.136
  69.1 2.0 broadcast_select_fusion.3
  72.0 1.4 copy.112.kplace_ref
  73.3 3.6 all-gather.9.cloned.1.call-done
  77.0 3.8 copy.114
  82.3 1.7 copy.109
  84.0 4.0 maximum_multiply_fusion
  88.0 30.9 %all-gather.7.cloned.1.call-done = bf16[2048,640]{0,1:T(8,128)(2,1)} async-done(((bf16[512,640]{0,1:T(8,128)(2,1)}), bf16[2048,640]{0,1:T(8,128)(2,1)}) %all-gather.7.cloned.1.call-update) | async-done | bytes 2621456 | tf_op jit(solution)/shard_map/all_gather | solution.py:191
  118.9 4.3 reshape.382
  123.2 5.3 copy.110
  128.5 2.8 fusion.43
  131.3 3.0 squeeze.34.value_t_ref
  134.4 4.8 fusion.41
  139.2 39.5 %attend.1 = (bf16[5,1,1536,64]{3,2,1,0:T(8,128)(2,1)S(1)}, f32[5,1,6,1,256]{4,3,2,1,0:T(1,128)S(1)}) custom-call(bf16[5,1,1536,64]{3,2,1,0:T(8,128)(2,1)S(1)} %bitcast.178, bf16[5,1,2048,64]{3,2,1,0:T(8,128)(2,1)S(1)} %bitcast.176, bf16[5,1,64,2048]{3,2,1,0:T(8,128)(2,1)S(1)} %squeeze.34.value_t_ref, s32[1,6,1,256]{3,2,1,0:T(1,128)S(1)} %broadcast_in_dim.8.qplace_ref, ...), custom_call_target="tpu_custom_call" | custom-call | flops 16106127360 | bytes 9175040 | tf_op jit(solution)/shard_map/attend/pallas_call | solution.py:94
  178.7 1.6 copy.113
  180.3 3.3 multiply_reduce_fusion.1
  183.6 13.3 %convolution_bitcast_fusion = f32[2,512,2560]{1,2,0:T(8,128)} fusion(bf16[2,960,2560]{2,1,0:T(8,128)(2,1)} %bitcast.215, f32[512,960]{0,1:T(8,128)S(1)} %get-tuple-element.148, f32[960]{0:T(1024)S(1)} %get-tuple-element.104, f32[512]{0:T(512)S(1)} %add_rsqrt_fusion), kind=kOutput, calls=%fused_computation.1 | convolution fusion | flops 5034639360 | bytes 22288128 | tf_op jit(solution)/shard_map/rd,bde->bre/dot_general | solution.py:187
  196.9 27.8 %all-gather.13.cloned.1.call-done = bf16[2560,960]{1,0:T(8,128)(2,1)} async-done(((bf16[320,960]{1,0:T(8,128)(2,1)}), bf16[2560,960]{1,0:T(8,128)(2,1)}) %all-gather.13.cloned.1.call-update) | async-done | bytes 4915216 | tf_op jit(solution)/shard_map/all_gather | solution.py:191
  224.7 10.3 %fusion.15 = (bf16[1,512,2560]{1,2,0:T(8,128)(2,1)S(1)}, bf16[1,512,2560]{1,2,0:T(8,128)(2,1)S(1)}, bf16[512,2560]{0,1:T(8,128)(2,1)}) fusion(f32[2,512,2560]{1,2,0:T(8,128)} %convolution_bitcast_fusion, bf16[2560,960]{1,0:T(8,128)(2,1)} %all-gather.13.cloned.1.call-done, bf16[512,960]{0,1:T(8,128)(2,1)S(1)} %copy-done.17), kind=kOutput, calls=%fused_computation.31 | convolution fusion | flops 2536243200 | bytes 24248320 | tf_op jit(solution)/shard_map/rd,ed->re/dot_general | solution.py:187
  235.0 5.5 fusion.23
  240.5 8.0 %convolution_convert_fusion = bf16[2,2560,960]{1,2,0:T(8,128)(2,1)} fusion(bf16[1,512,2560]{1,2,0:T(8,128)(2,1)S(1)} %get-tuple-element.110, bf16[1,512,2560]{1,2,0:T(8,128)(2,1)S(1)} %get-tuple-element.109, f32[512,960]{0,1:T(8,128)S(1)} %get-tuple-element.148, f32[960]{0:T(1024)S(1)} %get-tuple-element.104, f32[512]{0:T(512)S(1)} %add_rsqrt_fusion), kind=kOutput, calls=%fused_computation | convolution fusion | flops 5042176000 | bytes 17045248 | tf_op jit(solution)/shard_map/rd,bre->bde/dot_general | solution.py:187
  250.1 2.1 bitcast_convert_fusion
  252.2 1.2 convert_bitcast_fusion.1
  253.4 2.5 copy.119
  255.9 6.1 convolution_convert_fusion.1
  262.0 7.9 %copy.131 = bf16[2560,960]{1,0:T(8,128)(2,1)} copy(bf16[2560,960]{0,1:T(8,128)(2,1)} %convolution_convert_fusion.1) | data formatting | bytes 9830400
  273.0 2.8 copy.120
  275.8 1.2 copy-done.4
  277.1 68.4 %attend_back.1 = (f32[5,1,1536,64]{3,2,1,0:T(8,128)}, f32[5,1,2048,64]{3,2,1,0:T(8,128)}, f32[5,1,2048,64]{3,2,1,0:T(8,128)}) custom-call(bf16[5,1,1536,64]{3,2,1,0:T(8,128)(2,1)S(1)} %bitcast.179, bf16[5,1,2048,64]{3,2,1,0:T(8,128)(2,1)} %bitcast.177, bf16[5,1,64,2048]{3,2,1,0:T(8,128)(2,1)S(1)} %squeeze.37.key_t_ref, bf16[5,1,2048,64]{3,2,1,0:T(8,128)(2,1)} %bitcast.197, ...), custom_call_target="tpu_custom_call" | custom-call | flops 40265318400 | bytes 18350080 | tf_op jit(solution)/shard_map/attend_back/pallas_call | solution.py:123
  345.4 3.0 convert.62
  349.8 3.4 maximum_bitcast_fusion
  353.2 6.1 copy.124
  359.4 2.3 copy.141
  361.7 1.5 copy.132
  363.2 7.7 %reduce-scatter.12.cloned.1.call-done = bf16[240,480]{1,0:T(8,128)(2,1)} async-done(((bf16[1920,480]{1,0:T(8,128)(2,1)}), bf16[240,480]{1,0:T(8,128)(2,1)}) %reduce-scatter.12.cloned.1.call-update) | async-done | bytes 230416 | tf_op jit(solution)/shard_map/reduce_scatter | solution.py:195
  370.8 81.9 %reduce-scatter.10.cloned.1.call-done = bf16[240,2560]{1,0:T(8,128)(2,1)} async-done(((bf16[1920,2560]{1,0:T(8,128)(2,1)}), bf16[240,2560]{1,0:T(8,128)(2,1)}) %reduce-scatter.10.cloned.1.call-update) | async-done | bytes 1228816 | tf_op jit(solution)/shard_map/reduce_scatter | solution.py:195
  452.8 7.5 %fusion.42 = (f32[512,15,32]{2,0,1:T(8,128)}, f32[512,15,32]{2,0,1:T(8,128)}) fusion(f32[512,15,64]{2,0,1:T(8,128)} %bitcast.183), kind=kLoop, calls=%fused_computation.117 | loop fusion | bytes 3932160 | tf_op jit(solution)/shard_map/slice | solution.py:167
  460.3 2.9 copy.139
  463.2 2.7 copy.138
  467.9 27.4 %reduce-scatter.14.cloned.1.call-done = bf16[512,640]{0,1:T(8,128)(2,1)} async-done(((bf16[2048,640]{0,1:T(8,128)(2,1)}), bf16[512,640]{0,1:T(8,128)(2,1)}) %reduce-scatter.14.cloned.1.call-update) | async-done | bytes 655376 | tf_op jit(solution)/shard_map/reduce_scatter | solution.py:195
  499.2 3.4 fusion.21
  502.7 3.2 convert_bitcast_fusion
  505.9 3.4 copy.125
  509.3 4.4 concatenate.87
  513.8 2.1 pad_maximum_fusion.3
  515.9 71.2 %all-reduce.6.cloned.1.call-done = (bf16[320,960]{1,0:T(8,128)(2,1)}, bf16[240,2560]{1,0:T(8,128)(2,1)}, bf16[240,480]{1,0:T(8,128)(2,1)}) async-done(((bf16[320,960]{1,0:T(8,128)(2,1)}, bf16[240,2560]{1,0:T(8,128)(2,1)}, bf16[240,480]{1,0:T(8,128)(2,1)}), (bf16[320,960]{1,0:T(8,128)(2,1)}, bf16[240,2560]{1,0:T(8,128)(2,1)}, bf16[240,480]{1,0:T(8,128)(2,1)})) %all-reduce.6.cloned.1.call-update) | async-done | bytes 2073616 | tf_op jit(solution)/shard_map/psum | solution.py:385
  587.1 3.6 copy.133
  590.9 1.3 copy-done.6
  592.2 7.4 %add_convert_fusion = bf16[512,960]{0,1:T(8,128)(2,1)} fusion(f32[512,960]{0,1:T(8,128)S(1)} %copy-done.6, bf16[512,2560]{0,1:T(8,128)(2,1)} %get-tuple-element.111, bf16[2560,960]{1,0:T(8,128)(2,1)} %all-gather.13.cloned.1.call-done), kind=kOutput, calls=%fused_computation.49 | convolution fusion | flops 2517565440 | bytes 10485760 | tf_op jit(solution)/shard_map/re,ed->rd/dot_general | solution.py:187
  600.1 2.3 fusion.20
  603.6 35.1 %reduce-scatter.18.cloned.1.call-done = bf16[240,801]{1,0:T(8,128)(2,1)} async-done(((bf16[1920,801]{1,0:T(8,128)(2,1)}), bf16[240,801]{1,0:T(8,128)(2,1)}) %reduce-scatter.18.cloned.1.call-update) | async-done | bytes 384496
  638.7 1.9 copy.134
  640.7 1.4 broadcast_select_fusion.2
  642.4 2.0 copy.128
  644.4 34.2 %all-reduce.4.cloned.1.call-done = bf16[240,801]{0,1:T(8,128)(2,1)} async-done(((bf16[240,801]{0,1:T(8,128)(2,1)}), bf16[240,801]{0,1:T(8,128)(2,1)}) %all-reduce.4.cloned.1.call-update) | async-done | bytes 384496 | tf_op jit(solution)/shard_map/psum | solution.py:388
  678.6 4.3 select_convert_fusion
  685.2 1.3 copy.127
  (166 shorter events, 28.2 us)
Async XLA Ops:
  7.2 4.1 copy-start.27
  7.2 40.0 %all-gather.15.cloned.1.call-start = ((), (), s32[]{:S(2)}) async-start(), calls=%async_computation.13 | async-start | bytes 3723264 | tf_op jit(solution)/shard_map/all_gather | solution.py:191
  9.2 3.1 copy-start.35
  9.2 3.2 copy-start.13
  11.3 65.7 %all-gather.9.cloned.1.call-start = ((), (), s32[]{:S(2)}) async-start(), calls=%async_computation.6 | async-start | bytes 2211840 | tf_op jit(solution)/shard_map/all_gather | solution.py:191
  12.2 106.7 %all-gather.7.cloned.1.call-start = ((), (), s32[]{:S(2)}) async-start(), calls=%async_computation.5 | async-start | bytes 3276800 | tf_op jit(solution)/shard_map/all_gather | solution.py:191
  12.6 41.1 %copy-start.32 = (f32[512]{0:T(512)}, f32[512]{0:T(512)S(1)}, u32[]{:S(2)}) copy-start(f32[512]{0:T(512)S(1)} %add_rsqrt_fusion.1) | copy-start | bytes 6148
  13.7 67.2 %copy-start.21 = (f32[512,32]{0,1:T(8,128)}, f32[512,32]{0,1:T(8,128)S(1)}, u32[]{:S(2)}) copy-start(f32[512,32]{0,1:T(8,128)S(1)} %get-tuple-element.146) | copy-start | bytes 196612
  53.2 1.8 copy-start.11
  53.2 1.9 copy-start.14
  53.7 1.2 copy-start.30
  57.4 0.8 copy-start.26
  59.3 124.3 %all-gather.11.cloned.1.call-start = ((), (), s32[]{:S(2)}) async-start(), calls=%async_computation.7 | async-start | bytes 11059200 | tf_op jit(solution)/shard_map/all_gather | solution.py:191
  61.9 162.8 %all-gather.13.cloned.1.call-start = ((), (), s32[]{:S(2)}) async-start(), calls=%async_computation.8 | async-start | bytes 5898240 | tf_op jit(solution)/shard_map/all_gather | solution.py:191
  71.2 290.5 %reduce-scatter.16.cloned.1.call-start = ((), (), s32[]{:S(2)}) async-start(), calls=%async_computation.14 | async-start | bytes 5898240
  134.3 4.9 copy-start.1
  134.3 4.9 copy-start.3
  139.2 39.5 %copy-start = (bf16[1,5,1,4,512,64]{5,4,3,1,2,0:T(8,128)(2,1)}, bf16[1,5,1,4,512,64]{5,4,3,1,2,0:T(8,128)(2,1)S(1)}, u32[]{:S(2)}) copy-start(bf16[1,5,1,4,512,64]{5,4,3,1,2,0:T(8,128)(2,1)S(1)} %get-tuple-element.113) | copy-start | bytes 3932164
  183.6 64.9 %copy-start.5 = (f32[512,960]{0,1:T(8,128)}, f32[512,960]{0,1:T(8,128)S(1)}, u32[]{:S(2)}) copy-start(f32[512,960]{0,1:T(8,128)S(1)} %get-tuple-element.148) | copy-start | bytes 5898244
  183.6 41.1 %copy-start.17 = (bf16[512,960]{0,1:T(8,128)(2,1)S(1)}, bf16[512,960]{0,1:T(8,128)(2,1)}, u32[]{:S(2)}) copy-start(bf16[512,960]{0,1:T(8,128)(2,1)} %param.23) | copy-start | bytes 2949124
  224.7 10.3 %copy-start.34 = (bf16[1920,2560]{1,0:T(8,128)(2,1)S(1)}, bf16[1920,2560]{1,0:T(8,128)(2,1)}, u32[]{:S(2)}) copy-start(bf16[1920,2560]{1,0:T(8,128)(2,1)} %all-gather.11.cloned.1.call-done) | copy-start | bytes 29491204
  240.5 8.0 %copy-start.7 = (f32[512,960,1]{0,1,2:T(8,128)}, f32[512,960,1]{0,1,2:T(8,128)S(1)}, u32[]{:S(2)}) copy-start(f32[512,960,1]{0,1,2:T(8,128)S(1)} %get-tuple-element.149) | copy-start | bytes 5898244
  248.5 1.5 copy-start.20
  250.1 2.1 copy-start.23
  270.0 100.9 %reduce-scatter.12.cloned.1.call-start = ((), (), s32[]{:S(2)}) async-start(), calls=%async_computation.10 | async-start | bytes 2211840 | tf_op jit(solution)/shard_map/reduce_scatter | solution.py:195
  270.7 1.3 copy-start.9
  270.7 182.0 %reduce-scatter.10.cloned.1.call-start = ((), (), s32[]{:S(2)}) async-start(), calls=%async_computation.9 | async-start | bytes 11059200 | tf_op jit(solution)/shard_map/reduce_scatter | solution.py:195
  271.5 223.8 %reduce-scatter.14.cloned.1.call-start = ((), (), s32[]{:S(2)}) async-start(), calls=%async_computation.11 | async-start | bytes 3276800 | tf_op jit(solution)/shard_map/reduce_scatter | solution.py:195
  273.0 2.8 copy-start.2
  275.8 1.2 copy-start.4
  345.4 4.0 copy-start.10
  452.7 134.3 %all-reduce.6.cloned.1.call-start = ((), (), s32[]{:S(2)}) async-start(), calls=%async_computation.16 | async-start | bytes 4259840 | tf_op jit(solution)/shard_map/psum | solution.py:385
  463.2 2.8 copy-start.22
  463.2 2.8 copy-start.25
  467.5 171.3 %reduce-scatter.18.cloned.1.call-start = ((), (), s32[]{:S(2)}) async-start(), calls=%async_computation.15 | async-start | bytes 3870720
  496.6 1.4 copy-start.15
  496.6 2.5 copy-start.12
  496.6 2.5 copy-start.31
  496.7 2.5 copy-start.33
  496.8 5.8 copy-start.24
  590.6 1.5 copy-start.6
  590.6 8.9 %copy-start.29 = (bf16[240,480]{1,0:T(8,128)(2,1)S(1)}, bf16[240,480]{1,0:T(8,128)(2,1)}, u32[]{:S(2)}) copy-start(bf16[240,480]{1,0:T(8,128)(2,1)} %get-tuple-element.42) | copy-start | bytes 691204
  590.7 9.4 %copy-start.16 = (bf16[512,960]{0,1:T(8,128)(2,1)S(1)}, bf16[512,960]{0,1:T(8,128)(2,1)}, u32[]{:S(2)}) copy-start(bf16[512,960]{0,1:T(8,128)(2,1)} %param.12) | copy-start | bytes 2949124
  590.7 88.0 %all-reduce.4.cloned.1.call-start = ((), (), s32[]{:S(2)}) async-start(), calls=%async_computation.12 | async-start | bytes 827392 | tf_op jit(solution)/shard_map/psum | solution.py:388
  592.2 7.9 %copy-start.8 = (f32[512,960,1]{0,1,2:T(8,128)S(1)}, f32[512,960,1]{0,1,2:T(8,128)}, u32[]{:S(2)}) copy-start(f32[512,960,1]{0,1,2:T(8,128)} %copy-done.7) | copy-start | bytes 5898244
  592.2 7.9 %copy-start.18 = (bf16[512,960]{0,1:T(8,128)(2,1)S(1)}, bf16[512,960]{0,1:T(8,128)(2,1)}, u32[]{:S(2)}) copy-start(bf16[512,960]{0,1:T(8,128)(2,1)} %param.23) | copy-start | bytes 2949124
  592.2 7.9 %copy-start.19 = (f32[512,960,1]{0,1,2:T(8,128)S(1)}, f32[512,960,1]{0,1,2:T(8,128)}, u32[]{:S(2)}) copy-start(f32[512,960,1]{0,1,2:T(8,128)} %get-tuple-element.150) | copy-start | bytes 5898244
  599.5 2.9 collective-permute-start.1
  599.6 41.2 %collective-permute-start.3 = (bf16[320,960]{1,0:T(8,128)(2,1)}, bf16[320,960]{1,0:T(8,128)(2,1)}, u32[]{:S(2)}, u32[]{:S(2)}) collective-permute-start(bf16[320,960]{1,0:T(8,128)(2,1)} %get-tuple-element.44), channel_id=1, source_target_pairs={{0,1},{1,0},{2,3},{3,2},{4,5},{5,4},{6,7},{7,6},{8,9},{9,8},{10,11... | collective-permute-start | bytes 1843208 | tf_op jit(solution)/shard_map/ppermute | solution.py:199
  600.1 78.6 %collective-permute-start.2 = (bf16[240,2560]{1,0:T(8,128)(2,1)}, bf16[240,2560]{1,0:T(8,128)(2,1)}, u32[]{:S(2)}, u32[]{:S(2)}) collective-permute-start(bf16[240,2560]{1,0:T(8,128)(2,1)} %get-tuple-element.43), channel_id=1, source_target_pairs={{0,1},{1,0},{2,3},{3,2},{4,5},{5,4},{6,7},{7,6},{8,9},{9,8},{10,11... | collective-permute-start | bytes 3686408 | tf_op jit(solution)/shard_map/ppermute | solution.py:199
  678.6 4.3 copy-start.28
  678.6 4.3 collective-permute-start
Sparse Core Ops, SparseCore 0:
  11.4 35.7 all-gather.14
  49.6 27.3 all-gather.8
  79.4 39.4 all-gather.6
  120.7 60.4 all-gather.10
  183.5 41.1 all-gather.12
  270.1 56.5 reduce-scatter.15
  330.5 40.2 reduce-scatter.11
  374.4 78.2 reduce-scatter.9
  455.7 39.5 reduce-scatter.13
  498.3 88.7 all-reduce.5
  590.8 47.9 reduce-scatter.17
  641.6 36.9 all-reduce.3
